TPU v7x, 128 devices: a whole 4x4x4 slice. The times are simulated.
128 devices in a mesh: dp: 8 (over x_lo, y), seq: 16 (over x_hi, z, core).
Axes of the slice: x: 4 (x_hi: 2, x_lo: 2; x = x_hi * 2 + x_lo), y: 4, z: 4, core: 2. Of those that a mesh axis runs over, the one named last changes fastest.
Arguments:
- q_time: bfloat16 [8, 16, 256, 16, 128], P('dp', 'seq'), may hold values from -100 to 100
- k_time: bfloat16 [8, 16, 256, 16, 128], P('dp', 'seq'), may hold values from -12 to 12
- v_time: bfloat16 [8, 16, 256, 16, 128], P('dp', 'seq'), may hold values from -6 to 6
- q_space: bfloat16 [8, 16, 256, 16, 128], P('dp', 'seq'), may hold values from -100 to 100
- k_space: bfloat16 [8, 16, 256, 16, 128], P('dp', 'seq'), may hold values from -12 to 12
- audio_now: bfloat16 [8, 1024, 1024], P('dp', 'seq'), may hold values from -6 to 6
- audio_earlier: bfloat16 [8, 1024, 1024], P('dp', 'seq'), may hold values from -6 to 6
- cotangent: bfloat16 [8, 1024, 4096], P('dp', 'seq'), may hold values from -6 to 6
- audio_weight: bfloat16 [1024, 4096], replicated, may hold values from -0.1875 to 0.1875
Outputs:
- mixed: bfloat16 [8, 16, 256, 16, 128], P('dp', 'seq')
- weight_grad: float32 [1024, 4096], P(('dp', 'seq'))
All inputs are finite; a program needn't handle non-finite values.
Results may differ from a plain program's by a relative error of at most 0.013.
Values may be sent and summed in bfloat16 or wider, within the bound.
A program may use at most 128 MiB of HBM per device.

v0:
```python
import math

import jax
import jax.numpy as jnp
from jax import lax
from jax.sharding import PartitionSpec as P


def normalize(scores):
    row_max = jnp.max(scores, axis=-1, keepdims=True)
    expo = jnp.exp(scores - row_max)
    return (expo / jnp.sum(expo, axis=-1, keepdims=True)).astype(jnp.bfloat16)


def local(
    q_time, k_time, v_time, q_space, k_space, audio_now, audio_earlier, cotangent, audio_weight
):
    f32 = jnp.float32
    head_count = q_time.shape[3]
    head_dim = q_time.shape[4]
    factor = 1.0 / math.sqrt(head_dim)
    queries = lax.all_to_all(q_time, "seq", split_axis=2, concat_axis=1, tiled=True)
    key_rows = lax.all_to_all(k_time, "seq", split_axis=2, concat_axis=1, tiled=True)
    values = lax.all_to_all(v_time, "seq", split_axis=2, concat_axis=1, tiled=True)
    scores = (
        jnp.einsum("cfshd,cgshd->cshfg", queries, key_rows, preferred_element_type=f32) * factor
    )
    weights = normalize(scores)
    result = jnp.einsum("cshfg,cgshd->cfshd", weights, values, preferred_element_type=f32)
    by_position = (values.astype(f32) + result).astype(jnp.bfloat16)
    hidden = lax.all_to_all(by_position, "seq", split_axis=1, concat_axis=2, tiled=True)
    projected = jnp.dot(audio_now[0], audio_weight, preferred_element_type=f32).astype(jnp.bfloat16)
    audio_kv = lax.all_gather(projected, "seq", axis=0, tiled=True)
    audio_kv = audio_kv.reshape(audio_kv.shape[0], 2, head_count, head_dim)
    audio_keys = audio_kv[:, 0]
    audio_values = audio_kv[:, 1]

    def per_frame(inputs):
        queries, key_rows, values = inputs
        scores = jnp.einsum("shd,thd->hst", queries, key_rows, preferred_element_type=f32) * factor
        spatial = jnp.einsum("hst,thd->shd", normalize(scores), values, preferred_element_type=f32)
        cross_scores = (
            jnp.einsum("shd,ahd->hsa", queries, audio_keys, preferred_element_type=f32) * factor
        )
        cross_mix = jnp.einsum(
            "hsa,ahd->shd", normalize(cross_scores), audio_values, preferred_element_type=f32
        )
        return (values.astype(f32) + spatial + cross_mix).astype(jnp.bfloat16)

    mixed = lax.map(per_frame, (q_space[0], k_space[0], hidden[0]))[None]
    earlier = audio_earlier[0]
    cotan_rows = cotangent[0]
    weight_grad = lax.psum_scatter(
        lax.dot_general(earlier, cotan_rows, (((0,), (0,)), ((), ())), preferred_element_type=f32),
        ("dp", "seq"),
        scatter_dimension=0,
        tiled=True,
    )
    return (mixed, weight_grad)


def solution(mesh):
    placed = (
        P("dp", "seq", None, None, None),
        P("dp", "seq", None, None, None),
        P("dp", "seq", None, None, None),
        P("dp", "seq", None, None, None),
        P("dp", "seq", None, None, None),
        P("dp", "seq", None),
        P("dp", "seq", None),
        P("dp", "seq", None),
        P(),
    )
    return jax.shard_map(
        local,
        mesh=mesh,
        in_specs=placed,
        out_specs=(P("dp", "seq", None, None, None), P(("dp", "seq"), None)),
        check_vma=False,
    )
```

profile of v0, /device:TPU:1, one launch (start us, length us, event | category | flops | bytes accessed | tf_op | source)
XLA Modules:
  0.0 754.2 jit_solution(15602643762734840516)
XLA Ops:
  8.1 5.9 convolution_convert_fusion
  14.1 8.1 %fusion.35 = f32[1024,4096]{1,0:T(8,128)} fusion(bf16[1,64,4096]{2,1,0:T(8,128)(2,1)S(1)} %copy-done.8, bf16[1,64,1024]{2,1,0:T(8,128)(2,1)S(1)} %copy-done.9), kind=kOutput, calls=%fused_computation.41 | convolution fusion | flops 536870912 | bytes 17432576 | tf_op jit(solution)/shard_map/dot_general | solution.py:54
  22.2 1.2 copy-done.3
  23.4 29.6 %all_to_all.16 = bf16[1,1,256,16,128]{4,3,1,0,2:T(8,128)(2,1)} all-to-all(bf16[1,1,256,16,128]{4,3,1,0,2:T(8,128)(2,1)S(1)} %bitcast.86), channel_id=1, replica_groups=mesh['dp'=8,'seq'=16] {'seq'}, dimensions={2} | all-to-all | bytes 2097152 | tf_op jit(solution)/shard_map/all_to_all | solution.py:22
  53.0 27.6 %all_to_all.17 = bf16[1,1,256,16,128]{4,3,1,0,2:T(8,128)(2,1)S(1)} all-to-all(bf16[1,1,256,16,128]{4,3,1,0,2:T(8,128)(2,1)S(1)} %bitcast.87), channel_id=1, replica_groups=mesh['dp'=8,'seq'=16] {'seq'}, dimensions={2} | all-to-all | bytes 2097152 | tf_op jit(solution)/shard_map/all_to_all | solution.py:24
  80.6 6.3 all-to-all-start.2
  86.9 1.6 convert.1
  88.5 22.7 %all-to-all-done.2 = bf16[1,1,256,16,128]{4,3,1,0,2:T(8,128)(2,1)} async-done(((bf16[1,1,256,16,128]{4,3,1,0,2:T(8,128)(2,1)}), bf16[1,1,256,16,128]{4,3,1,0,2:T(8,128)(2,1)}, u32[]{:S(2)}, u32[]{:S(2)}) %all-to-all-start.2) | async-done | bytes 1048608 | tf_op jit(solution)/shard_map/all_to_all | solution.py:23
  111.2 4.4 fusion.63
  115.7 4.2 fusion.15
  119.8 1.2 copy.45
  121.1 4.1 all-to-all-start.3
  125.9 3.0 fusion.68
  128.9 15.0 %all-to-all-done.3 = bf16[1,16,16,16,128]{4,3,2,0,1:T(8,128)(2,1)S(1)} async-done(((bf16[1,16,16,16,128]{4,3,2,0,1:T(8,128)(2,1)}), bf16[1,16,16,16,128]{4,3,2,0,1:T(8,128)(2,1)S(1)}, u32[]{:S(2)}, u32[]{:S(2)}) %all-to-all-start.3) | async-done | bytes 1048608 | tf_op jit(solution)/shard_map/all_to_all | solution.py:31
  144.0 0.8 copy.46
  144.8 4.4 fusion.18
  149.2 9.4 %copy.61 = bf16[128,8,32,128]{3,2,1,0:T(8,128)(2,1)} copy(bf16[128,8,32,128]{3,1,2,0:T(8,128)(2,1)} %bitcast.82) | data formatting | bytes 16777216
  158.6 6.3 fusion.61
  165.0 6.8 copy.59
  171.7 10.3 %fusion.10 = f32[16,1024,256]{2,1,0:T(8,128)} fusion(bf16[1024,1,16,128]{3,2,1,0:T(8,128)(2,1)} %get-tuple-element.30, bf16[256,16,128]{2,1,0:T(8,128)(2,1)S(1)} %bitcast.81), kind=kOutput, calls=%fused_computation.13 | convolution fusion | flops 1073741824 | bytes 22020096 | tf_op jit(solution)/shard_map/while/body/eval_jaxpr/shd,ahd->hsa/dot_general | solution.py:43
  182.0 12.7 %fusion.62 = f32[16,256]{1,0:T(8,128)S(1)} fusion(f32[16,1024,256]{2,1,0:T(8,128)} %fusion.10), kind=kOutput, calls=%fused_computation.51 | output fusion | flops 16778240 | bytes 16793600 | tf_op jit(solution)/shard_map/while/body/eval_jaxpr/sub | solution.py:11
  194.8 16.7 %fusion.22 = bf16[1,1,256,16,128]{2,4,3,1,0:T(8,128)(2,1)S(1)} fusion(f32[16,256]{1,0:T(8,128)S(1)} %fusion.62, bf16[1024,1,16,128]{0,3,2,1:T(8,128)(2,1)} %copy.59, f32[16,128,256]{2,1,0:T(8,128)} %fusion.18, bf16[256,16,128]{0,2,1:T(8,128)(2,1)S(1)} %copy-done.6, f32[16,1024,256]{2,1,0:T(8,128)} %fusion.10), kind=kOutput, calls=%fused_computation.30 | convolution fusion | flops 1096815616 | bytes 25182208 | tf_op jit(solution)/shard_map/while/body/eval_jaxpr/hsa,ahd->shd/dot_general | solution.py:45
  211.5 1.8 copy.55
  213.3 533.5 %reduce-scatter.2.cloned.1.call-done = f32[8,4096]{1,0:T(8,128)} async-done(((f32[1024,4096]{1,0:T(8,128)}), f32[8,4096]{1,0:T(8,128)}) %reduce-scatter.2.cloned.1.call-update) | async-done | bytes 131088 | tf_op jit(solution)/shard_map/reduce_scatter | solution.py:53
  (25 shorter events, 0.9 us)
Async XLA Ops:
  8.0 117.2 %copy-start = (bf16[1,1,256,16,128]{4,3,2,1,0:T(8,128)(2,1)S(1)}, bf16[1,1,256,16,128]{4,3,2,1,0:T(8,128)(2,1)}, u32[]{:S(2)}) copy-start(bf16[1,1,256,16,128]{4,3,2,1,0:T(8,128)(2,1)} %param.13) | copy-start | bytes 3145732
  8.0 6.1 copy-start.8
  8.0 6.1 copy-start.9
  8.0 141.1 %all-gather.2.cloned.1.call-start = ((), (), s32[]{:S(2)}) async-start(), calls=%async_computation.5 | async-start | bytes 8912896 | tf_op jit(solution)/shard_map/all_gather | solution.py:33
  14.0 732.7 %reduce-scatter.2.cloned.1.call-start = ((), (), s32[]{:S(2)}) async-start(), calls=%async_computation.6 | async-start | bytes 16908288 | tf_op jit(solution)/shard_map/reduce_scatter | solution.py:53
  22.2 1.2 copy-start.3
  22.2 30.8 %copy-start.4 = (bf16[1,1,256,16,128]{4,3,2,1,0:T(8,128)(2,1)S(1)}, bf16[1,1,256,16,128]{4,3,2,1,0:T(8,128)(2,1)}, u32[]{:S(2)}) copy-start(bf16[1,1,256,16,128]{4,3,2,1,0:T(8,128)(2,1)} %param.11) | copy-start | bytes 3145732
  80.6 30.6 %copy-start.7 = (bf16[1,1,256,16,128]{4,3,1,0,2:T(8,128)(2,1)S(1)}, bf16[1,1,256,16,128]{4,3,1,0,2:T(8,128)(2,1)}, u32[]{:S(2)}) copy-start(bf16[1,1,256,16,128]{4,3,1,0,2:T(8,128)(2,1)} %all_to_all.16) | copy-start | bytes 3145732
  80.6 30.6 %all-to-all-start.2 = ((bf16[1,1,256,16,128]{4,3,1,0,2:T(8,128)(2,1)}), bf16[1,1,256,16,128]{4,3,1,0,2:T(8,128)(2,1)}, u32[]{:S(2)}, u32[]{:S(2)}) async-start(bf16[1,1,256,16,128]{4,3,1,0,2:T(8,128)(2,1)} %bitcast.88), calls=%async_computation.2 | async-start | bytes 2097152 | tf_op jit(solution)/shard_map/all_to_all | solution.py:23
  119.8 5.3 copy-start.2
  121.1 22.9 %all-to-all-start.3 = ((bf16[1,16,16,16,128]{4,3,2,0,1:T(8,128)(2,1)}), bf16[1,16,16,16,128]{4,3,2,0,1:T(8,128)(2,1)S(1)}, u32[]{:S(2)}, u32[]{:S(2)}) async-start(bf16[1,16,16,16,128]{4,3,2,0,1:T(8,128)(2,1)} %copy.45), calls=%async_computation.3 | async-start | bytes 2097152 | tf_op jit(solution)/shard_map/all_to_all | solution.py:31
  144.8 4.4 copy-start.5
  182.0 12.8 %copy-start.6 = (bf16[256,16,128]{0,2,1:T(8,128)(2,1)S(1)}, bf16[256,16,128]{0,2,1:T(8,128)(2,1)}, u32[]{:S(2)}) copy-start(bf16[256,16,128]{0,2,1:T(8,128)(2,1)} %copy-done.5) | copy-start | bytes 3145732
  194.7 552.0 %copy-start.1 = (bf16[1,1,256,16,128]{4,3,2,1,0:T(8,128)(2,1)S(1)}, bf16[1,1,256,16,128]{4,3,2,1,0:T(8,128)(2,1)}, u32[]{:S(2)}) copy-start(bf16[1,1,256,16,128]{4,3,2,1,0:T(8,128)(2,1)} %param.13) | copy-start | bytes 3145732
Sparse Core Ops, SparseCore 0:
  14.1 100.7 all-gather.1
Sparse Core Ops, SparseCore 1:
  22.3 724.4 reduce-scatter.1
where the time goes:
time: 760 us; the launch traced here: 754 us
  waiting for transfers between devices  571 us (75%)
  blocking collectives  57.2 us (8%)
  matrix products  54.7 us (7%)
  local copies, waits for them, and re-layouts  27.6 us (4%)
  other arithmetic  17.4 us (2%)
  between operations  15.6 us (2%)
  starting transfers between devices  10.5 us (1%)
    reduce_scatter x1, waiting for transfers between devices, local(): lax.psum_scatter(lax.dot_general(earlier, cotan_rows, (((0,), (0,)), ((),...  533 us
    all_to_all x1, blocking collectives, local(): lax.all_to_all(q_time, 'seq', split_axis=2, concat_axis=1, tiled=True)  29.6 us
    all_to_all x1, blocking collectives, local(): lax.all_to_all(v_time, 'seq', split_axis=2, concat_axis=1, tiled=True)  27.6 us
    all_to_all x1, waiting for transfers between devices, local(): lax.all_to_all(k_time, 'seq', split_axis=2, concat_axis=1, tiled=True)  22.7 us
    unnamed x23, local copies, waits for them, and re-layouts  19.2 us
    dot_general x1, matrix products, per_frame(): jnp.einsum('hsa,ahd->shd', normalize(cross_scores), audio_values, preferr...  16.7 us
    sub x2, other arithmetic, normalize(): expo = jnp.exp(scores - row_max)  15.8 us
  transfers between devices with their start and end apart: 4, of which 3 were waited for; matrix products, arithmetic and copies ran while one was open for 12% of the time, Pallas kernels for 0%

commit v1 on v0

v1 whole, which is shorter than its diff:
```python
import functools
import math

import jax
import jax.numpy as jnp
from jax import lax
from jax.experimental import pallas as pl
from jax.experimental.pallas import tpu as pltpu
from jax.sharding import PartitionSpec as P

MESH = pl.DeviceIdType.MESH
F32 = jnp.float32
BF16 = jnp.bfloat16
HEADS, HD, SPOTS, FRAMES = 16, 128, 256, 16
CHUNKS = 4
PART = SPOTS // FRAMES // CHUNKS
EXP_SCALE = math.log2(math.e) / math.sqrt(HD)
NEG = -1e30


def dot(a, b):
    return lax.dot_general(a, b, (((1,), (0,)), ((), ())), preferred_element_type=F32)


def dot_nt(a, b):
    return lax.dot_general(a, b, (((1,), (1,)), ((), ())), preferred_element_type=F32)


def dot_tn(a, b):
    return lax.dot_general(a, b, (((0,), (0,)), ((), ())), preferred_element_type=F32)


def softmax(scores):
    row_max = jnp.max(scores, axis=-1, keepdims=True)
    expo = jnp.exp2((scores - row_max) * EXP_SCALE)
    return (expo * (1.0 / jnp.sum(expo, axis=-1, keepdims=True))).astype(BF16)


def kernel(
    q_time, k_time, v_time, q_space, k_space, audio_now, audio_earlier, cotangent, weight,
    mixed, grad,
    arrived, back, hidden, q_raw, k_raw, q_heads, k_heads, hid_heads, spatial, cross, out_heads,
    audio, w_vmem, kv, earlier, cotan, part_z, from_z, part_x, from_x, part_y, rows, bias, perm,
    local_sem, qkv_send, qkv_recv, hid_send, hid_recv, aud_send, aud_recv, grad_send, grad_recv,
    out_sem,
):
    dp = lax.axis_index("dp")
    me = lax.axis_index("seq")
    x_lo, y = dp // 4, dp % 4
    x_hi, z, core = me // 8, (me // 2) % 4, me % 2
    x = x_hi * 2 + x_lo
    line = y * 2 + core

    def at(x_, y_, z_, c_):
        return ((x_ % 2) * 4 + y_, (x_ // 2) * 8 + z_ * 2 + c_)

    def send(src, dst, send_sem, recv_sem, device):
        pltpu.make_async_remote_copy(
            src, dst, send_sem, recv_sem, device_id=device, device_id_type=MESH
        ).start()

    def local(src, dst, sem):
        pltpu.make_async_copy(src, dst, sem).start()

    def wait(ref, sem):
        pltpu.make_async_copy(ref, ref, sem).wait()

    def seq_peer(step):
        far = step % 2
        rest = step // 2
        return ((x_hi + far) % 2) * 8 + ((z + rest // 2) % 4) * 2 + (core + rest) % 2

    def y_peer(step):
        return (y + step // 2) % 4, (core + step) % 2

    for c in range(CHUNKS):
        local(q_space.at[:, c], q_raw.at[c], local_sem.at[0])
        local(k_space.at[:, c], k_raw.at[c], local_sem.at[1])
        for t, ref in enumerate((q_time, k_time, v_time)):
            local(ref.at[me, c], arrived.at[c, t, me], qkv_recv.at[c])
    local(weight, w_vmem, local_sem.at[2])
    local(audio_now, audio.at[me // 2, core], local_sem.at[3])
    local(audio_earlier, earlier.at[line], grad_recv.at[0])
    local(cotangent.at[:, pl.ds(pl.multiple_of(line * 512, 512), 512)], cotan.at[line], grad_recv.at[1])

    barrier = pltpu.get_barrier_semaphore()

    def greet(device):
        pl.semaphore_signal(barrier, inc=1, device_id=device, device_id_type=MESH)

    def greet_seq(step, carry):
        greet((dp, seq_peer(step)))
        return carry

    lax.fori_loop(1, 16, greet_seq, 0)

    def greet_y(step, carry):
        y_, c_ = y_peer(step)
        greet(at(x, y_, z, c_))
        return carry

    lax.fori_loop(2, 8, greet_y, 0)
    greet(at((x + 1) % 4, y, z, core))
    greet(at((x + 3) % 4, y, z, core))
    pl.semaphore_wait(barrier, 23)

    mine = audio.at[me // 2, core]
    send(audio_now, mine, aud_send.at[0], aud_recv.at[0], at((x + 2) % 4, y, z, core))
    for d in (1, 3, 2):
        send(audio_now, mine, aud_send.at[0], aud_recv.at[1], at(x, y, (z + d) % 4, core))

    def send_qkv(c):
        def body(step, carry):
            peer = seq_peer(step)
            for t, ref in enumerate((q_time, k_time, v_time)):
                send(ref.at[peer, c], arrived.at[c, t, me], qkv_send.at[t], qkv_recv.at[c], (dp, peer))
            return carry

        lax.fori_loop(1, 16, body, 0)

    send_qkv(0)

    def send_y(step, carry):
        y_, c_ = y_peer(step)
        to = at(x, y_, z, c_)
        cols = pl.ds(pl.multiple_of((y_ * 2 + c_) * 512, 512), 512)
        send(audio_earlier, earlier.at[line], grad_send.at[0], grad_recv.at[0], to)
        send(cotangent.at[:, cols], cotan.at[line], grad_send.at[1], grad_recv.at[1], to)
        return carry

    lax.fori_loop(1, 8, send_y, 0)
    for c in range(1, CHUNKS):
        send_qkv(c)

    row = lax.broadcasted_iota(jnp.int32, (256, 256), 0)
    col = lax.broadcasted_iota(jnp.int32, (256, 256), 1)
    bias[...] = jnp.where(row % 16 == col % 16, 0.0, NEG).astype(F32)
    perm[...] = jnp.where(col == (row % 16) * 16 + row // 16, 1.0, 0.0).astype(BF16)

    def to_heads(src, dst, first, count):
        def body(i, carry):
            block = src[i // 4, pl.ds((i % 4) * (16 // PART), 16 // PART)].reshape(256, HD)
            turned = dot(perm[...], block).astype(BF16).reshape(HEADS, 16, HD)
            dst[:, pl.ds(pl.multiple_of(i * 16, 16), 16), :] = turned
            return carry

        lax.fori_loop(first, first + count, body, 0)

    wait(q_raw, local_sem.at[0])
    to_heads(q_raw, q_heads, 0, 16)
    wait(k_raw, local_sem.at[1])
    to_heads(k_raw, k_heads, 0, 16)

    wait(mine, aud_recv.at[0])
    other = ((x_hi + 1) % 2) * 4 + z
    theirs = audio.at[other, core]
    for d in (1, 3, 2):
        send(theirs, theirs, aud_send.at[0], aud_recv.at[1], at(x, y, (z + d) % 4, core))

    def spatial_scores(h, carry):
        spatial[h] = softmax(dot_nt(q_heads[h], k_heads[h]))
        return carry

    lax.fori_loop(0, HEADS, spatial_scores, 0)

    wait(earlier, grad_recv.at[0])
    wait(cotan, grad_recv.at[1])

    def partial_rows(i, carry):
        x_lo_, y_ = i // 4, i % 4
        lanes = pl.ds(pl.multiple_of(i * 128, 128), 128)
        block = dot_tn(earlier[:, :, lanes].reshape(512, 128), cotan[...].reshape(512, 512))
        block = block.astype(BF16).reshape(2, 4, 16, 512)
        for a in range(2):
            for b in range(4):
                part_z[b, a * 2 + x_lo_, y_] = block[a, b]
        return carry

    lax.fori_loop(0, 8, partial_rows, 0)
    for d in (1, 3, 2):
        z_ = (z + d) % 4
        send(part_z.at[z_], from_z.at[z], grad_send.at[2], grad_recv.at[2], at(x, y, z_, core))
    local(part_z.at[z], from_z.at[z], grad_recv.at[2])

    wait(audio_now, local_sem.at[3])
    wait(audio.at[pl.ds(0, 6), 0], aud_recv.at[1])
    side = audio.at[:, core]
    send(side, side, aud_send.at[1], aud_recv.at[2], at(x, y, z, 1 - core))

    def temporal(c):
        wait(arrived.at[c], qkv_recv.at[c])

        def body(s, carry):
            queries = arrived[c, 0, :, s].reshape(256, HD)
            key_rows = arrived[c, 1, :, s].reshape(256, HD)
            values = arrived[c, 2, :, s].reshape(256, HD)
            weights = softmax(dot_nt(queries, key_rows) + bias[...])
            result = values.astype(F32) + dot(weights, values)
            back[c, :, s] = result.astype(BF16).reshape(FRAMES, HEADS, HD)
            return carry

        lax.fori_loop(0, PART, body, 0)

        def go(step, carry):
            peer = seq_peer(step)
            send(back.at[c, peer], hidden.at[c, me], hid_send.at[0], hid_recv.at[c], (dp, peer))
            return carry

        lax.fori_loop(1, 16, go, 0)
        local(back.at[c, me], hidden.at[c, me], hid_recv.at[c])

    def audio_pair(p, carry):
        tokens = audio[...].reshape(1024, 1024)
        lanes = pl.ds(pl.multiple_of(p * 256, 256), 256)
        more = pl.ds(pl.multiple_of(2048 + p * 256, 256), 256)
        kv[0] = dot(tokens, w_vmem[:, lanes]).astype(BF16)
        kv[1] = dot(tokens, w_vmem[:, more]).astype(BF16)
        for i in range(2):
            span = slice(i * 128, (i + 1) * 128)
            weights = softmax(dot_nt(q_heads[p * 2 + i], kv[0, :, span]))
            cross[p * 2 + i] = dot(weights, kv[1, :, span])
        return carry

    wait(w_vmem, local_sem.at[2])
    wait(audio.at[:, 0], aud_recv.at[2])
    lax.fori_loop(0, 2, audio_pair, 0)
    temporal(0)
    lax.fori_loop(2, 4, audio_pair, 0)

    wait(from_z, grad_recv.at[2])
    for x_ in range(4):
        total = from_z[0, x_].astype(F32)
        for z_ in range(1, 4):
            total += from_z[z_, x_].astype(F32)
        part_x[x_] = total.astype(BF16)
    for d in (2, 1, 3):
        x_ = (x + d) % 4
        send(part_x.at[x_], from_x.at[x], grad_send.at[3], grad_recv.at[3], at(x_, y, z, core))
    local(part_x.at[x], from_x.at[x], grad_recv.at[3])

    temporal(1)
    lax.fori_loop(4, 6, audio_pair, 0)
    temporal(2)
    lax.fori_loop(6, 8, audio_pair, 0)

    wait(from_x, grad_recv.at[3])
    for y_ in range(4):
        total = from_x[0, y_].astype(F32)
        for x_ in range(1, 4):
            total += from_x[x_, y_].astype(F32)
        part_y[y_] = total.reshape(2, 8, 512)
    cols = pl.ds(pl.multiple_of(line * 512, 512), 512)

    def send_rows(step, carry):
        y_, c_ = y_peer(step)
        send(part_y.at[y_, c_], rows.at[:, cols], grad_send.at[4], grad_recv.at[4], at(x, y_, z, c_))
        return carry

    lax.fori_loop(1, 8, send_rows, 0)
    local(part_y.at[y, core], rows.at[:, cols], grad_recv.at[4])

    temporal(3)

    wait(rows, grad_recv.at[4])
    local(rows, grad, out_sem.at[1])

    for c in range(CHUNKS):
        wait(hidden.at[c], hid_recv.at[c])
        to_heads(hidden, hid_heads, c * 4, 4)

    def finish(h, carry):
        values = hid_heads[h]
        result = values.astype(F32) + dot(spatial[h], values) + cross[h]
        out_heads[h] = result.astype(BF16)
        local(out_heads.at[h], mixed.at[h], out_sem.at[0])
        return carry

    lax.fori_loop(0, HEADS, finish, 0)

    wait(mixed, out_sem.at[0])
    wait(grad, out_sem.at[1])
    for t, ref in enumerate((q_time, k_time, v_time)):
        wait(ref.at[pl.ds(0, 15)], qkv_send.at[t])
    wait(back.at[:, pl.ds(0, 15)], hid_send.at[0])
    wait(audio.at[pl.ds(0, 7), 0], aud_send.at[0])
    wait(audio.at[:, 0], aud_send.at[1])
    wait(earlier.at[pl.ds(0, 7)], grad_send.at[0])
    wait(cotan.at[pl.ds(0, 7)], grad_send.at[1])
    wait(from_z.at[pl.ds(0, 3)], grad_send.at[2])
    wait(from_x.at[pl.ds(0, 3)], grad_send.at[3])
    wait(rows.at[:, pl.ds(0, 7 * 512)], grad_send.at[4])


def local(
    q_time, k_time, v_time, q_space, k_space, audio_now, audio_earlier, cotangent, audio_weight
):
    split = (FRAMES, CHUNKS, PART, HEADS, HD)
    vmem = lambda shape, dtype: pltpu.VMEM(shape, dtype)
    dma = lambda n: pltpu.SemaphoreType.DMA((n,))
    anywhere = pl.BlockSpec(memory_space=pl.ANY)
    mixed, grad = pl.pallas_call(
        kernel,
        out_shape=(
            jax.ShapeDtypeStruct((HEADS, SPOTS, HD), BF16),
            jax.ShapeDtypeStruct((8, 4096), F32),
        ),
        in_specs=[anywhere] * 9,
        out_specs=(anywhere, anywhere),
        scratch_shapes=[
            vmem((CHUNKS, 3, FRAMES, PART, HEADS, HD), BF16),
            vmem((CHUNKS, FRAMES, PART, HEADS, HD), BF16),
            vmem((CHUNKS, FRAMES, PART, HEADS, HD), BF16),
            vmem((CHUNKS, FRAMES, PART, HEADS, HD), BF16),
            vmem((CHUNKS, FRAMES, PART, HEADS, HD), BF16),
            vmem((HEADS, SPOTS, HD), BF16),
            vmem((HEADS, SPOTS, HD), BF16),
            vmem((HEADS, SPOTS, HD), BF16),
            vmem((HEADS, SPOTS, SPOTS), BF16),
            vmem((HEADS, SPOTS, HD), F32),
            vmem((HEADS, SPOTS, HD), BF16),
            vmem((8, 2, 64, 1024), BF16),
            vmem((1024, 4096), BF16),
            vmem((2, 1024, 256), BF16),
            vmem((8, 64, 1024), BF16),
            vmem((8, 64, 512), BF16),
            vmem((4, 4, 4, 16, 512), BF16),
            vmem((4, 4, 4, 16, 512), BF16),
            vmem((4, 4, 16, 512), BF16),
            vmem((4, 4, 16, 512), BF16),
            vmem((4, 2, 8, 512), F32),
            vmem((8, 4096), F32),
            vmem((256, 256), F32),
            vmem((256, 256), BF16),
            dma(4), dma(3), dma(CHUNKS), dma(1), dma(CHUNKS), dma(2), dma(3), dma(5), dma(5), dma(2),
        ],
        compiler_params=pltpu.CompilerParams(
            collective_id=0, has_side_effects=True, vmem_limit_bytes=52 * 2**20
        ),
        name="block",
    )(
        q_time.reshape(split), k_time.reshape(split), v_time.reshape(split),
        q_space.reshape(split), k_space.reshape(split),
        audio_now[0], audio_earlier[0], cotangent[0], audio_weight,
    )
    mixed = mixed.reshape(HEADS, CHUNKS, FRAMES, PART, HD).transpose(2, 1, 3, 0, 4)
    return mixed.reshape(1, 1, SPOTS, HEADS, HD), grad


def solution(mesh):
    placed = (
        P("dp", "seq", None, None, None),
        P("dp", "seq", None, None, None),
        P("dp", "seq", None, None, None),
        P("dp", "seq", None, None, None),
        P("dp", "seq", None, None, None),
        P("dp", "seq", None),
        P("dp", "seq", None),
        P("dp", "seq", None),
        P(),
    )
    return jax.shard_map(
        local,
        mesh=mesh,
        in_specs=placed,
        out_specs=(P("dp", "seq", None, None, None), P(("dp", "seq"), None)),
        check_vma=False,
    )
```

time: 760 us -> 107 us (0.14)
  waiting for transfers between devices: 571 us -> 0 us
  Pallas kernels: 0 us -> 101 us
  blocking collectives: 57.2 us -> 0 us
  matrix products: 54.7 us -> 0 us
  local copies, waits for them, and re-layouts: 27.6 us -> 5.69 us
  other arithmetic: 17.4 us -> 0 us
  between operations: 15.6 us -> 0.65 us
  starting transfers between devices: 10.5 us -> 0 us
    reduce_scatter x1 -> x0, waiting for transfers between devices: 533 us -> none  [local(): lax.psum_scatter(lax.dot_general(earlier, cotan_rows, (((0,), (0,)), ((),...]
    pallas_call x0 -> x1, Pallas kernels: none -> 101 us  [local(): pl.pallas_call(kernel, out_shape=(jax.ShapeDtypeStruct((HEADS, SPOTS, HD)...]
    all_to_all x2 -> x0, blocking collectives: 57.2 us -> none  [the longest x1 29.6 us: local(): lax.all_to_all(q_time, 'seq', split_axis=2, concat_axis=1, tiled=True)]
    dot_general x7 -> x0, matrix products: 50.3 us -> none  [the longest x1 16.7 us: per_frame(): jnp.einsum('hsa,ahd->shd', normalize(cross_scores), audio_values, preferr...]
    all_to_all x2 -> x0, waiting for transfers between devices: 37.7 us -> none  [the longest x1 22.7 us: local(): lax.all_to_all(k_time, 'seq', split_axis=2, concat_axis=1, tiled=True)]
    sub x2 -> x0, other arithmetic: 15.8 us -> none  [normalize(): expo = jnp.exp(scores - row_max)]
    unnamed x23 -> x7, local copies, waits for them, and re-layouts: 19.2 us -> 3.5 us
    all_to_all x2 -> x0, starting transfers between devices: 10.4 us -> none  [the longest x1 6.3 us: local(): lax.all_to_all(k_time, 'seq', split_axis=2, concat_axis=1, tiled=True)]
  transfers between devices with their start and end apart: 4 -> 0, of which waited for: 3 -> 0; matrix products, arithmetic and copies ran while one was open for 12% -> 0% of each run, Pallas kernels for 0% -> 0%
where the time goes in v1:
time: 107 us
  Pallas kernels  101 us (94%)
  local copies, waits for them, and re-layouts  5.69 us (5%)
    pallas_call x1, Pallas kernels, local(): pl.pallas_call(kernel, out_shape=(jax.ShapeDtypeStruct((HEADS, SPOTS, HD)...  101 us
    unnamed x7, local copies, waits for them, and re-layouts  3.5 us
    transpose x1, local copies, waits for them, and re-layouts, local(): mixed.reshape(HEADS, CHUNKS, FRAMES, PART, HD).transpose(2, 1, 3, 0, 4)  2.19 us

profile of v1, /device:TPU:1, one launch (start us, length us, event | category | flops | bytes accessed | tf_op | source)
XLA Modules:
  0.0 107.1 jit_solution(17802322828981965495)
XLA Ops:
  0.6 0.0 copy-start
  0.6 1.0 copy-done
  1.7 0.0 copy-start.1
  1.7 0.9 copy-done.1
  2.6 0.0 copy-start.2
  2.6 0.9 copy-done.2
  3.5 100.8 %block.1 = (bf16[16,256,128]{2,1,0:T(8,128)(2,1)S(1)}, f32[8,4096]{1,0:T(8,128)S(1)}) custom-call(bf16[16,4,4,16,128]{4,3,2,1,0:T(8,128)(2,1)} %bitcast.16, bf16[16,4,4,16,128]{4,3,2,1,0:T(8,128)(2,1)} %bitcast.17, bf16[16,4,4,16,128]{4,3,2,1,0:T(8,128)(2,1)} %bitcast.18, bf16[16,4,4,16,128]{4,3,2,1,0:T(8,128)(2,1)} %bitcast.19, ...), custom_call_target="tpu_custom_call" | custom-call | tf_op jit(solution)/shard_map/block/pallas_call | solution.py:301
  104.3 2.2 %copy.11 = bf16[16,4,4,16,128]{4,3,2,1,0:T(8,128)(2,1)} copy(bf16[16,4,4,16,128]{4,2,0,1,3:T(4,128)(2,1)S(1)} %bitcast.12) | data formatting | bytes 2097152 | tf_op jit(solution)/shard_map/transpose | solution.py:345
  106.4 0.7 copy.13
Async XLA Ops:
  0.6 1.0 copy-start
  1.7 0.9 copy-start.1
  2.6 0.9 copy-start.2

commit v2 on v1

--- a/solution.py
+++ b/solution.py
@@ -33,14 +33,14 @@
 def softmax(scores):
     row_max = jnp.max(scores, axis=-1, keepdims=True)
     expo = jnp.exp2((scores - row_max) * EXP_SCALE)
-    return (expo * (1.0 / jnp.sum(expo, axis=-1, keepdims=True))).astype(BF16)
+    return expo, jnp.sum(expo, axis=-1, keepdims=True)
 
 
 def kernel(
     q_time, k_time, v_time, q_space, k_space, audio_now, audio_earlier, cotangent, weight,
     mixed, grad,
     arrived, back, hidden, q_raw, k_raw, q_heads, k_heads, hid_heads, spatial, cross, out_heads,
-    audio, w_vmem, kv, earlier, cotan, part_z, from_z, part_x, from_x, part_y, rows, bias, perm,
+    audio, w_vmem, kv, earlier, cotan, part_x, from_x, part_z, from_z, part_y, rows, bias, perm,
     local_sem, qkv_send, qkv_recv, hid_send, hid_recv, aud_send, aud_recv, grad_send, grad_recv,
     out_sem,
 ):
@@ -129,39 +129,74 @@
         return carry
 
     lax.fori_loop(1, 8, send_y, 0)
-    for c in range(1, CHUNKS):
-        send_qkv(c)
 
     row = lax.broadcasted_iota(jnp.int32, (256, 256), 0)
     col = lax.broadcasted_iota(jnp.int32, (256, 256), 1)
     bias[...] = jnp.where(row % 16 == col % 16, 0.0, NEG).astype(F32)
     perm[...] = jnp.where(col == (row % 16) * 16 + row // 16, 1.0, 0.0).astype(BF16)
 
-    def to_heads(src, dst, first, count):
-        def body(i, carry):
-            block = src[i // 4, pl.ds((i % 4) * (16 // PART), 16 // PART)].reshape(256, HD)
-            turned = dot(perm[...], block).astype(BF16).reshape(HEADS, 16, HD)
-            dst[:, pl.ds(pl.multiple_of(i * 16, 16), 16), :] = turned
-            return carry
-
-        lax.fori_loop(first, first + count, body, 0)
+    def to_heads(src, dst, c):
+        blocks = jnp.concatenate(
+            [src[c, pl.ds(i * (16 // PART), 16 // PART)].reshape(256, HD) for i in range(4)], axis=1
+        )
+        turned = dot(perm[...], blocks).astype(BF16)
+        for i in range(4):
+            dst[:, pl.ds(pl.multiple_of(c * 64 + i * 16, 16), 16), :] = turned[
+                :, i * HD : (i + 1) * HD
+            ].reshape(HEADS, 16, HD)
+
+    def q_to_heads(c, carry):
+        to_heads(q_raw, q_heads, c)
+        return carry
+
+    def k_to_heads(c, carry):
+        to_heads(k_raw, k_heads, c)
+        return carry
 
     wait(q_raw, local_sem.at[0])
-    to_heads(q_raw, q_heads, 0, 16)
+    lax.fori_loop(0, CHUNKS, q_to_heads, 0)
     wait(k_raw, local_sem.at[1])
-    to_heads(k_raw, k_heads, 0, 16)
+    lax.fori_loop(0, CHUNKS, k_to_heads, 0)
 
     wait(mine, aud_recv.at[0])
     other = ((x_hi + 1) % 2) * 4 + z
     theirs = audio.at[other, core]
     for d in (1, 3, 2):
         send(theirs, theirs, aud_send.at[0], aud_recv.at[1], at(x, y, (z + d) % 4, core))
-
-    def spatial_scores(h, carry):
-        spatial[h] = softmax(dot_nt(q_heads[h], k_heads[h]))
-        return carry
-
-    lax.fori_loop(0, HEADS, spatial_scores, 0)
+    send_qkv(1)
+
+    def spatial_scores(i, carry):
+        for h in (2 * i, 2 * i + 1):
+            expo, total = softmax(dot_nt(q_heads[h], k_heads[h]))
+            spatial[h] = (expo * (1.0 / total)).astype(BF16)
+        return carry
+
+    lax.fori_loop(0, HEADS // 2, spatial_scores, 0)
+
+    def temporal(c):
+        wait(arrived.at[c], qkv_recv.at[c])
+
+        def attend(i, carry):
+            for s in (2 * i, 2 * i + 1):
+                queries = arrived[c, 0, :, s].reshape(256, HD)
+                key_rows = arrived[c, 1, :, s].reshape(256, HD)
+                values = arrived[c, 2, :, s].reshape(256, HD)
+                expo, total = softmax(dot_nt(queries, key_rows) + bias[...])
+                result = values.astype(F32) + dot(expo.astype(BF16), values) * (1.0 / total)
+                back[c, :, s] = result.astype(BF16).reshape(FRAMES, HEADS, HD)
+            return carry
+
+        lax.fori_loop(0, PART // 2, attend, 0)
+
+        def go(step, carry):
+            peer = seq_peer(step)
+            send(back.at[c, peer], hidden.at[c, me], hid_send.at[0], hid_recv.at[c], (dp, peer))
+            return carry
+
+        lax.fori_loop(1, 16, go, 0)
+        local(back.at[c, me], hidden.at[c, me], hid_recv.at[c])
+
+    temporal(0)
 
     wait(earlier, grad_recv.at[0])
     wait(cotan, grad_recv.at[1])
@@ -173,41 +208,23 @@
         block = block.astype(BF16).reshape(2, 4, 16, 512)
         for a in range(2):
             for b in range(4):
-                part_z[b, a * 2 + x_lo_, y_] = block[a, b]
+                part_x[a * 2 + x_lo_, b, y_] = block[a, b]
         return carry
 
     lax.fori_loop(0, 8, partial_rows, 0)
-    for d in (1, 3, 2):
-        z_ = (z + d) % 4
-        send(part_z.at[z_], from_z.at[z], grad_send.at[2], grad_recv.at[2], at(x, y, z_, core))
-    local(part_z.at[z], from_z.at[z], grad_recv.at[2])
+    for d in (2, 1, 3):
+        x_ = (x + d) % 4
+        send(part_x.at[x_], from_x.at[x], grad_send.at[2], grad_recv.at[2], at(x_, y, z, core))
+    local(part_x.at[x], from_x.at[x], grad_recv.at[2])
+    send_qkv(2)
 
     wait(audio_now, local_sem.at[3])
     wait(audio.at[pl.ds(0, 6), 0], aud_recv.at[1])
     side = audio.at[:, core]
     send(side, side, aud_send.at[1], aud_recv.at[2], at(x, y, z, 1 - core))
 
-    def temporal(c):
-        wait(arrived.at[c], qkv_recv.at[c])
-
-        def body(s, carry):
-            queries = arrived[c, 0, :, s].reshape(256, HD)
-            key_rows = arrived[c, 1, :, s].reshape(256, HD)
-            values = arrived[c, 2, :, s].reshape(256, HD)
-            weights = softmax(dot_nt(queries, key_rows) + bias[...])
-            result = values.astype(F32) + dot(weights, values)
-            back[c, :, s] = result.astype(BF16).reshape(FRAMES, HEADS, HD)
-            return carry
-
-        lax.fori_loop(0, PART, body, 0)
-
-        def go(step, carry):
-            peer = seq_peer(step)
-            send(back.at[c, peer], hidden.at[c, me], hid_send.at[0], hid_recv.at[c], (dp, peer))
-            return carry
-
-        lax.fori_loop(1, 16, go, 0)
-        local(back.at[c, me], hidden.at[c, me], hid_recv.at[c])
+    temporal(1)
+    send_qkv(3)
 
     def audio_pair(p, carry):
         tokens = audio[...].reshape(1024, 1024)
@@ -217,37 +234,34 @@
         kv[1] = dot(tokens, w_vmem[:, more]).astype(BF16)
         for i in range(2):
             span = slice(i * 128, (i + 1) * 128)
-            weights = softmax(dot_nt(q_heads[p * 2 + i], kv[0, :, span]))
-            cross[p * 2 + i] = dot(weights, kv[1, :, span])
+            expo, total = softmax(dot_nt(q_heads[p * 2 + i], kv[0, :, span]))
+            cross[p * 2 + i] = dot(expo.astype(BF16), kv[1, :, span]) * (1.0 / total)
         return carry
 
     wait(w_vmem, local_sem.at[2])
     wait(audio.at[:, 0], aud_recv.at[2])
-    lax.fori_loop(0, 2, audio_pair, 0)
-    temporal(0)
-    lax.fori_loop(2, 4, audio_pair, 0)
-
-    wait(from_z, grad_recv.at[2])
-    for x_ in range(4):
-        total = from_z[0, x_].astype(F32)
+    lax.fori_loop(0, 4, audio_pair, 0)
+    temporal(2)
+
+    wait(from_x, grad_recv.at[2])
+    for z_ in range(4):
+        total = from_x[0, z_].astype(F32)
+        for x_ in range(1, 4):
+            total += from_x[x_, z_].astype(F32)
+        part_z[z_] = total.astype(BF16)
+    for d in (1, 3, 2):
+        z_ = (z + d) % 4
+        send(part_z.at[z_], from_z.at[z], grad_send.at[3], grad_recv.at[3], at(x, y, z_, core))
+    local(part_z.at[z], from_z.at[z], grad_recv.at[3])
+
+    lax.fori_loop(4, 8, audio_pair, 0)
+    temporal(3)
+
+    wait(from_z, grad_recv.at[3])
+    for y_ in range(4):
+        total = from_z[0, y_].astype(F32)
         for z_ in range(1, 4):
-            total += from_z[z_, x_].astype(F32)
-        part_x[x_] = total.astype(BF16)
-    for d in (2, 1, 3):
-        x_ = (x + d) % 4
-        send(part_x.at[x_], from_x.at[x], grad_send.at[3], grad_recv.at[3], at(x_, y, z, core))
-    local(part_x.at[x], from_x.at[x], grad_recv.at[3])
-
-    temporal(1)
-    lax.fori_loop(4, 6, audio_pair, 0)
-    temporal(2)
-    lax.fori_loop(6, 8, audio_pair, 0)
-
-    wait(from_x, grad_recv.at[3])
-    for y_ in range(4):
-        total = from_x[0, y_].astype(F32)
-        for x_ in range(1, 4):
-            total += from_x[x_, y_].astype(F32)
+            total += from_z[z_, y_].astype(F32)
         part_y[y_] = total.reshape(2, 8, 512)
     cols = pl.ds(pl.multiple_of(line * 512, 512), 512)
 
@@ -259,23 +273,21 @@
     lax.fori_loop(1, 8, send_rows, 0)
     local(part_y.at[y, core], rows.at[:, cols], grad_recv.at[4])
 
-    temporal(3)
-
+    for c in range(CHUNKS):
+        wait(hidden.at[c], hid_recv.at[c])
+        to_heads(hidden, hid_heads, c)
+
+    def finish(i, carry):
+        for h in [4 * i + j for j in range(4)]:
+            values = hid_heads[h]
+            result = values.astype(F32) + dot(spatial[h], values) + cross[h]
+            out_heads[h] = result.astype(BF16)
+            local(out_heads.at[h], mixed.at[h], out_sem.at[0])
+        return carry
+
+    lax.fori_loop(0, HEADS // 4, finish, 0)
     wait(rows, grad_recv.at[4])
     local(rows, grad, out_sem.at[1])
-
-    for c in range(CHUNKS):
-        wait(hidden.at[c], hid_recv.at[c])
-        to_heads(hidden, hid_heads, c * 4, 4)
-
-    def finish(h, carry):
-        values = hid_heads[h]
-        result = values.astype(F32) + dot(spatial[h], values) + cross[h]
-        out_heads[h] = result.astype(BF16)
-        local(out_heads.at[h], mixed.at[h], out_sem.at[0])
-        return carry
-
-    lax.fori_loop(0, HEADS, finish, 0)
 
     wait(mixed, out_sem.at[0])
     wait(grad, out_sem.at[1])
@@ -286,8 +298,8 @@
     wait(audio.at[:, 0], aud_send.at[1])
     wait(earlier.at[pl.ds(0, 7)], grad_send.at[0])
     wait(cotan.at[pl.ds(0, 7)], grad_send.at[1])
-    wait(from_z.at[pl.ds(0, 3)], grad_send.at[2])
-    wait(from_x.at[pl.ds(0, 3)], grad_send.at[3])
+    wait(from_x.at[pl.ds(0, 3)], grad_send.at[2])
+    wait(from_z.at[pl.ds(0, 3)], grad_send.at[3])
     wait(rows.at[:, pl.ds(0, 7 * 512)], grad_send.at[4])
 
 
@@ -334,7 +346,7 @@
             dma(4), dma(3), dma(CHUNKS), dma(1), dma(CHUNKS), dma(2), dma(3), dma(5), dma(5), dma(2),
         ],
         compiler_params=pltpu.CompilerParams(
-            collective_id=0, has_side_effects=True, vmem_limit_bytes=52 * 2**20
+            collective_id=0, has_side_effects=True, vmem_limit_bytes=62 * 2**20
         ),
         name="block",
     )(

time: 107 us -> 84 us (0.79)
  Pallas kernels: 101 us -> 78.2 us
    pallas_call x1, Pallas kernels: 101 us -> 78.2 us  [local(): pl.pallas_call(kernel, out_shape=(jax.ShapeDtypeStruct((HEADS, SPOTS, HD)...]
    unnamed x7 -> x1, local copies, waits for them, and re-layouts: 3.5 us -> 1.57 us
    transpose x1, local copies, waits for them, and re-layouts: 2.19 us -> 3.41 us  [local(): mixed.reshape(HEADS, CHUNKS, FRAMES, PART, HD).transpose(2, 1, 3, 0, 4)]
where the time goes in v2:
time: 84 us; the launch traced here: 83.9 us
  Pallas kernels  78.2 us (93%)
  local copies, waits for them, and re-layouts  4.98 us (6%)
    pallas_call x1, Pallas kernels, local(): pl.pallas_call(kernel, out_shape=(jax.ShapeDtypeStruct((HEADS, SPOTS, HD)...  78.2 us
    transpose x1, local copies, waits for them, and re-layouts, local(): mixed.reshape(HEADS, CHUNKS, FRAMES, PART, HD).transpose(2, 1, 3, 0, 4)  3.41 us

profile of v2, /device:TPU:1, one launch (start us, length us, event | category | flops | bytes accessed | tf_op | source)
XLA Modules:
  0.0 83.9 jit_solution(7416995196482216921)
XLA Ops:
  0.6 78.2 %block.1 = (bf16[16,256,128]{2,1,0:T(8,128)(2,1)}, f32[8,4096]{1,0:T(8,128)}) custom-call(bf16[16,4,4,16,128]{4,3,2,1,0:T(8,128)(2,1)} %bitcast.12, bf16[16,4,4,16,128]{4,3,2,1,0:T(8,128)(2,1)} %bitcast.13, bf16[16,4,4,16,128]{4,3,2,1,0:T(8,128)(2,1)} %bitcast.14, bf16[16,4,4,16,128]{4,3,2,1,0:T(8,128)(2,1)} %bitcast.15, ...), custom_call_target="tpu_custom_call" | custom-call | tf_op jit(solution)/shard_map/block/pallas_call | solution.py:313
  78.9 3.4 %copy.11 = bf16[16,4,4,16,128]{4,3,2,1,0:T(8,128)(2,1)} copy(bf16[16,4,4,16,128]{4,2,0,1,3:T(4,128)(2,1)} %bitcast.18) | data formatting | bytes 2097152 | tf_op jit(solution)/shard_map/transpose | solution.py:357
  82.3 1.6 %copy.13 = f32[8,4096]{1,0:T(8,128)} copy(f32[8,4096]{1,0:T(8,128)} %get-tuple-element.9) | data formatting | bytes 262144

commit v3 on v2

--- a/solution.py
+++ b/solution.py
@@ -16,6 +16,7 @@
 PART = SPOTS // FRAMES // CHUNKS
 EXP_SCALE = math.log2(math.e) / math.sqrt(HD)
 NEG = -1e30
+LIMIT = 52 * 2**20
 
 
 def dot(a, b):
@@ -38,11 +39,10 @@
 
 def kernel(
     q_time, k_time, v_time, q_space, k_space, audio_now, audio_earlier, cotangent, weight,
-    mixed, grad,
-    arrived, back, hidden, q_raw, k_raw, q_heads, k_heads, hid_heads, spatial, cross, out_heads,
-    audio, w_vmem, kv, earlier, cotan, part_x, from_x, part_z, from_z, part_y, rows, bias, perm,
+    out_heads, rows_out,
+    arrived, back, hidden, q_raw, k_raw, q_heads, k_heads, hid_heads, spatial, cross,
+    audio, w_vmem, kv, earlier, cotan, part_x, relay, merged, from_x, part_z, from_z, part_y, rows, bias, perm,
     local_sem, qkv_send, qkv_recv, hid_send, hid_recv, aud_send, aud_recv, grad_send, grad_recv,
-    out_sem,
 ):
     dp = lax.axis_index("dp")
     me = lax.axis_index("seq")
@@ -66,13 +66,36 @@
         pltpu.make_async_copy(ref, ref, sem).wait()
 
     def seq_peer(step):
-        far = step % 2
-        rest = step // 2
-        return ((x_hi + far) % 2) * 8 + ((z + rest // 2) % 4) * 2 + (core + rest) % 2
+        pure = 1 - (step + 14) // 16
+        last = step // 14
+        mid = 1 - pure - last
+        far = pure + mid * (step % 2)
+        along = mid * (1 + (step // 2 + 2) % 3)
+        swap = pure * (step % 2) + mid * ((step + 4) // 6 % 2) + last
+        return ((x_hi + far) % 2) * 8 + ((z + along) % 4) * 2 + (core + swap) % 2
 
     def y_peer(step):
         return (y + step // 2) % 4, (core + step) % 2
 
+    barrier = pltpu.get_barrier_semaphore()
+
+    def greet(device):
+        pl.semaphore_signal(barrier, inc=1, device_id=device, device_id_type=MESH)
+
+    def greet_seq(step, carry):
+        greet((dp, seq_peer(step)))
+        return carry
+
+    lax.fori_loop(0, 15, greet_seq, 0)
+
+    def greet_y(step, carry):
+        y_, c_ = y_peer(step)
+        greet(at(x, y_, z, c_))
+        return carry
+
+    lax.fori_loop(2, 8, greet_y, 0)
+    greet(at((x + 1) % 4, y, z, core))
+    greet(at((x + 3) % 4, y, z, core))
     for c in range(CHUNKS):
         local(q_space.at[:, c], q_raw.at[c], local_sem.at[0])
         local(k_space.at[:, c], k_raw.at[c], local_sem.at[1])
@@ -80,28 +103,9 @@
             local(ref.at[me, c], arrived.at[c, t, me], qkv_recv.at[c])
     local(weight, w_vmem, local_sem.at[2])
     local(audio_now, audio.at[me // 2, core], local_sem.at[3])
-    local(audio_earlier, earlier.at[line], grad_recv.at[0])
+    local(audio_earlier, earlier.at[y, core], grad_recv.at[0])
     local(cotangent.at[:, pl.ds(pl.multiple_of(line * 512, 512), 512)], cotan.at[line], grad_recv.at[1])
 
-    barrier = pltpu.get_barrier_semaphore()
-
-    def greet(device):
-        pl.semaphore_signal(barrier, inc=1, device_id=device, device_id_type=MESH)
-
-    def greet_seq(step, carry):
-        greet((dp, seq_peer(step)))
-        return carry
-
-    lax.fori_loop(1, 16, greet_seq, 0)
-
-    def greet_y(step, carry):
-        y_, c_ = y_peer(step)
-        greet(at(x, y_, z, c_))
-        return carry
-
-    lax.fori_loop(2, 8, greet_y, 0)
-    greet(at((x + 1) % 4, y, z, core))
-    greet(at((x + 3) % 4, y, z, core))
     pl.semaphore_wait(barrier, 23)
 
     mine = audio.at[me // 2, core]
@@ -109,31 +113,34 @@
     for d in (1, 3, 2):
         send(audio_now, mine, aud_send.at[0], aud_recv.at[1], at(x, y, (z + d) % 4, core))
 
-    def send_qkv(c):
-        def body(step, carry):
-            peer = seq_peer(step)
+    def send_qkv(c, steps):
+        def one(peer):
             for t, ref in enumerate((q_time, k_time, v_time)):
                 send(ref.at[peer, c], arrived.at[c, t, me], qkv_send.at[t], qkv_recv.at[c], (dp, peer))
+
+        def body(step, carry):
+            one(seq_peer(step))
             return carry
 
-        lax.fori_loop(1, 16, body, 0)
-
-    send_qkv(0)
-
+        lax.fori_loop(steps[0], steps[1], body, 0)
+
+    send_qkv(0, (0, 2))
+    send_qkv(1, (0, 2))
     def send_y(step, carry):
         y_, c_ = y_peer(step)
         to = at(x, y_, z, c_)
         cols = pl.ds(pl.multiple_of((y_ * 2 + c_) * 512, 512), 512)
-        send(audio_earlier, earlier.at[line], grad_send.at[0], grad_recv.at[0], to)
         send(cotangent.at[:, cols], cotan.at[line], grad_send.at[1], grad_recv.at[1], to)
         return carry
 
+    for d in (1, 3, 2):
+        send(audio_earlier, earlier.at[y, core], grad_send.at[0], grad_recv.at[0], at(x, (y + d) % 4, z, core))
     lax.fori_loop(1, 8, send_y, 0)
 
     row = lax.broadcasted_iota(jnp.int32, (256, 256), 0)
     col = lax.broadcasted_iota(jnp.int32, (256, 256), 1)
     bias[...] = jnp.where(row % 16 == col % 16, 0.0, NEG).astype(F32)
-    perm[...] = jnp.where(col == (row % 16) * 16 + row // 16, 1.0, 0.0).astype(BF16)
+    perm[...] = permutation()
 
     def to_heads(src, dst, c):
         blocks = jnp.concatenate(
@@ -153,25 +160,11 @@
         to_heads(k_raw, k_heads, c)
         return carry
 
-    wait(q_raw, local_sem.at[0])
-    lax.fori_loop(0, CHUNKS, q_to_heads, 0)
-    wait(k_raw, local_sem.at[1])
-    lax.fori_loop(0, CHUNKS, k_to_heads, 0)
-
-    wait(mine, aud_recv.at[0])
-    other = ((x_hi + 1) % 2) * 4 + z
-    theirs = audio.at[other, core]
-    for d in (1, 3, 2):
-        send(theirs, theirs, aud_send.at[0], aud_recv.at[1], at(x, y, (z + d) % 4, core))
-    send_qkv(1)
-
     def spatial_scores(i, carry):
         for h in (2 * i, 2 * i + 1):
             expo, total = softmax(dot_nt(q_heads[h], k_heads[h]))
             spatial[h] = (expo * (1.0 / total)).astype(BF16)
         return carry
-
-    lax.fori_loop(0, HEADS // 2, spatial_scores, 0)
 
     def temporal(c):
         wait(arrived.at[c], qkv_recv.at[c])
@@ -193,38 +186,18 @@
             send(back.at[c, peer], hidden.at[c, me], hid_send.at[0], hid_recv.at[c], (dp, peer))
             return carry
 
-        lax.fori_loop(1, 16, go, 0)
+        lax.fori_loop(0, 15, go, 0)
         local(back.at[c, me], hidden.at[c, me], hid_recv.at[c])
-
-    temporal(0)
-
-    wait(earlier, grad_recv.at[0])
-    wait(cotan, grad_recv.at[1])
 
     def partial_rows(i, carry):
         x_lo_, y_ = i // 4, i % 4
         lanes = pl.ds(pl.multiple_of(i * 128, 128), 128)
-        block = dot_tn(earlier[:, :, lanes].reshape(512, 128), cotan[...].reshape(512, 512))
+        block = dot_tn(earlier[:, :, :, lanes].reshape(512, 128), cotan[...].reshape(512, 512))
         block = block.astype(BF16).reshape(2, 4, 16, 512)
         for a in range(2):
             for b in range(4):
                 part_x[a * 2 + x_lo_, b, y_] = block[a, b]
         return carry
-
-    lax.fori_loop(0, 8, partial_rows, 0)
-    for d in (2, 1, 3):
-        x_ = (x + d) % 4
-        send(part_x.at[x_], from_x.at[x], grad_send.at[2], grad_recv.at[2], at(x_, y, z, core))
-    local(part_x.at[x], from_x.at[x], grad_recv.at[2])
-    send_qkv(2)
-
-    wait(audio_now, local_sem.at[3])
-    wait(audio.at[pl.ds(0, 6), 0], aud_recv.at[1])
-    side = audio.at[:, core]
-    send(side, side, aud_send.at[1], aud_recv.at[2], at(x, y, z, 1 - core))
-
-    temporal(1)
-    send_qkv(3)
 
     def audio_pair(p, carry):
         tokens = audio[...].reshape(1024, 1024)
@@ -238,25 +211,61 @@
             cross[p * 2 + i] = dot(expo.astype(BF16), kv[1, :, span]) * (1.0 / total)
         return carry
 
+    wait(q_raw, local_sem.at[0])
+    lax.fori_loop(0, CHUNKS, q_to_heads, 0)
+    wait(k_raw, local_sem.at[1])
+    lax.fori_loop(0, CHUNKS, k_to_heads, 0)
+
+    wait(mine, aud_recv.at[0])
+    theirs = audio.at[((x_hi + 1) % 2) * 4 + z, core]
+    for d in (1, 3, 2):
+        send(theirs, theirs, aud_send.at[0], aud_recv.at[1], at(x, y, (z + d) % 4, core))
+    send_qkv(0, (2, 15))
+    lax.fori_loop(0, 8, spatial_scores, 0)
+    wait(earlier.at[:, 0], grad_recv.at[0])
+    half = earlier.at[:, core]
+    send(half, half, grad_send.at[5], grad_recv.at[5], at(x, y, z, 1 - core))
+    send_qkv(1, (2, 15))
+    wait(cotan, grad_recv.at[1])
+    wait(earlier.at[:, 0], grad_recv.at[5])
+    lax.fori_loop(0, 8, partial_rows, 0)
+
+    right, left = (x + 1) % 4, (x + 3) % 4
+    to_right, to_left = at(right, y, z, core), at(left, y, z, core)
+    early, late = pl.ds(0, 2), pl.ds(2, 2)
+    send(part_x.at[(x + 2) % 4, early], relay.at[0], grad_send.at[2], grad_recv.at[2], to_right)
+    send(part_x.at[(x + 2) % 4, late], relay.at[1], grad_send.at[2], grad_recv.at[2], to_left)
+    send(part_x.at[right, late], from_x.at[0, late], grad_send.at[2], grad_recv.at[6], to_right)
+    send(part_x.at[left, early], from_x.at[1, early], grad_send.at[2], grad_recv.at[6], to_left)
+    wait(audio_now, local_sem.at[3])
+    wait(audio.at[pl.ds(0, 6), 0], aud_recv.at[1])
+    side = audio.at[:, core]
+    send(side, side, aud_send.at[1], aud_recv.at[2], at(x, y, z, 1 - core))
+    send_qkv(2, (0, 15))
+    temporal(0)
+    wait(relay, grad_recv.at[2])
+    merged[0] = (part_x[right, early].astype(F32) + relay[0].astype(F32)).astype(BF16)
+    merged[1] = (part_x[left, late].astype(F32) + relay[1].astype(F32)).astype(BF16)
+    send(merged.at[0], from_x.at[0, early], grad_send.at[6], grad_recv.at[6], to_right)
+    send(merged.at[1], from_x.at[1, late], grad_send.at[6], grad_recv.at[6], to_left)
     wait(w_vmem, local_sem.at[2])
     wait(audio.at[:, 0], aud_recv.at[2])
-    lax.fori_loop(0, 4, audio_pair, 0)
-    temporal(2)
-
-    wait(from_x, grad_recv.at[2])
+    lax.fori_loop(0, 3, audio_pair, 0)
+    temporal(1)
+    send_qkv(3, (0, 15))
+    lax.fori_loop(3, 6, audio_pair, 0)
+    wait(from_x, grad_recv.at[6])
     for z_ in range(4):
-        total = from_x[0, z_].astype(F32)
-        for x_ in range(1, 4):
-            total += from_x[x_, z_].astype(F32)
+        total = part_x[x, z_].astype(F32) + from_x[0, z_].astype(F32) + from_x[1, z_].astype(F32)
         part_z[z_] = total.astype(BF16)
     for d in (1, 3, 2):
         z_ = (z + d) % 4
         send(part_z.at[z_], from_z.at[z], grad_send.at[3], grad_recv.at[3], at(x, y, z_, core))
     local(part_z.at[z], from_z.at[z], grad_recv.at[3])
 
-    lax.fori_loop(4, 8, audio_pair, 0)
+    temporal(2)
+    lax.fori_loop(6, 8, audio_pair, 0)
     temporal(3)
-
     wait(from_z, grad_recv.at[3])
     for y_ in range(4):
         total = from_z[0, y_].astype(F32)
@@ -282,25 +291,48 @@
             values = hid_heads[h]
             result = values.astype(F32) + dot(spatial[h], values) + cross[h]
             out_heads[h] = result.astype(BF16)
-            local(out_heads.at[h], mixed.at[h], out_sem.at[0])
         return carry
 
     lax.fori_loop(0, HEADS // 4, finish, 0)
     wait(rows, grad_recv.at[4])
-    local(rows, grad, out_sem.at[1])
-
-    wait(mixed, out_sem.at[0])
-    wait(grad, out_sem.at[1])
+    rows_out[...] = rows[...]
+
     for t, ref in enumerate((q_time, k_time, v_time)):
         wait(ref.at[pl.ds(0, 15)], qkv_send.at[t])
     wait(back.at[:, pl.ds(0, 15)], hid_send.at[0])
     wait(audio.at[pl.ds(0, 7), 0], aud_send.at[0])
     wait(audio.at[:, 0], aud_send.at[1])
-    wait(earlier.at[pl.ds(0, 7)], grad_send.at[0])
+    wait(earlier.at[pl.ds(0, 3), 0], grad_send.at[0])
+    wait(earlier.at[:, 0], grad_send.at[5])
+    wait(merged, grad_send.at[6])
     wait(cotan.at[pl.ds(0, 7)], grad_send.at[1])
-    wait(from_x.at[pl.ds(0, 3)], grad_send.at[2])
+    wait(from_x, grad_send.at[2])
     wait(from_z.at[pl.ds(0, 3)], grad_send.at[3])
     wait(rows.at[:, pl.ds(0, 7 * 512)], grad_send.at[4])
+
+
+def permutation():
+    row = lax.broadcasted_iota(jnp.int32, (256, 256), 0)
+    col = lax.broadcasted_iota(jnp.int32, (256, 256), 1)
+    return jnp.where(col == (row % 16) * 16 + row // 16, 1.0, 0.0).astype(BF16)
+
+
+def write_out(out_heads, rows, mixed, grad, turned, sem):
+    grad_copy = pltpu.make_async_copy(rows, grad, sem.at[0])
+    grad_copy.start()
+    perm = permutation()
+    for c in range(CHUNKS):
+        blocks = jnp.concatenate(
+            [out_heads[:, c * 64 + i * 16 : c * 64 + (i + 1) * 16, :].reshape(256, HD) for i in range(4)],
+            axis=1,
+        )
+        block = dot(perm, blocks).astype(BF16)
+        for i in range(4):
+            part = block[:, i * HD : (i + 1) * HD].reshape(16 // PART, PART, HEADS, HD)
+            turned[c, pl.ds(i * (16 // PART), 16 // PART)] = part
+        pltpu.make_async_copy(turned.at[c], mixed.at[:, c], sem.at[1]).start()
+    pltpu.make_async_copy(turned, turned, sem.at[1]).wait()
+    grad_copy.wait()
 
 
 def local(
@@ -310,14 +342,14 @@
     vmem = lambda shape, dtype: pltpu.VMEM(shape, dtype)
     dma = lambda n: pltpu.SemaphoreType.DMA((n,))
     anywhere = pl.BlockSpec(memory_space=pl.ANY)
-    mixed, grad = pl.pallas_call(
+    out_heads, rows = pl.pallas_call(
         kernel,
         out_shape=(
             jax.ShapeDtypeStruct((HEADS, SPOTS, HD), BF16),
             jax.ShapeDtypeStruct((8, 4096), F32),
         ),
         in_specs=[anywhere] * 9,
-        out_specs=(anywhere, anywhere),
+        out_specs=(pl.BlockSpec(memory_space=pltpu.VMEM),) * 2,
         scratch_shapes=[
             vmem((CHUNKS, 3, FRAMES, PART, HEADS, HD), BF16),
             vmem((CHUNKS, FRAMES, PART, HEADS, HD), BF16),
@@ -329,24 +361,25 @@
             vmem((HEADS, SPOTS, HD), BF16),
             vmem((HEADS, SPOTS, SPOTS), BF16),
             vmem((HEADS, SPOTS, HD), F32),
-            vmem((HEADS, SPOTS, HD), BF16),
             vmem((8, 2, 64, 1024), BF16),
             vmem((1024, 4096), BF16),
             vmem((2, 1024, 256), BF16),
-            vmem((8, 64, 1024), BF16),
+            vmem((4, 2, 64, 1024), BF16),
             vmem((8, 64, 512), BF16),
             vmem((4, 4, 4, 16, 512), BF16),
-            vmem((4, 4, 4, 16, 512), BF16),
+            vmem((2, 2, 4, 16, 512), BF16),
+            vmem((2, 2, 4, 16, 512), BF16),
+            vmem((2, 4, 4, 16, 512), BF16),
             vmem((4, 4, 16, 512), BF16),
             vmem((4, 4, 16, 512), BF16),
             vmem((4, 2, 8, 512), F32),
             vmem((8, 4096), F32),
             vmem((256, 256), F32),
             vmem((256, 256), BF16),
-            dma(4), dma(3), dma(CHUNKS), dma(1), dma(CHUNKS), dma(2), dma(3), dma(5), dma(5), dma(2),
+            dma(4), dma(3), dma(CHUNKS), dma(1), dma(CHUNKS), dma(2), dma(5), dma(7), dma(7),
         ],
         compiler_params=pltpu.CompilerParams(
-            collective_id=0, has_side_effects=True, vmem_limit_bytes=62 * 2**20
+            collective_id=0, has_side_effects=True, vmem_limit_bytes=LIMIT
         ),
         name="block",
     )(
@@ -354,7 +387,21 @@
         q_space.reshape(split), k_space.reshape(split),
         audio_now[0], audio_earlier[0], cotangent[0], audio_weight,
     )
-    mixed = mixed.reshape(HEADS, CHUNKS, FRAMES, PART, HD).transpose(2, 1, 3, 0, 4)
+    mixed, grad = pl.pallas_call(
+        write_out,
+        out_shape=(
+            jax.ShapeDtypeStruct((FRAMES, CHUNKS, PART, HEADS, HD), BF16),
+            jax.ShapeDtypeStruct((8, 4096), F32),
+        ),
+        in_specs=[pl.BlockSpec(memory_space=pltpu.VMEM)] * 2,
+        out_specs=(anywhere, anywhere),
+        scratch_shapes=[
+            vmem((CHUNKS, FRAMES, PART, HEADS, HD), BF16),
+            dma(2),
+        ],
+        compiler_params=pltpu.CompilerParams(vmem_limit_bytes=16 * 2**20),
+        name="write_out",
+    )(out_heads, rows)
     return mixed.reshape(1, 1, SPOTS, HEADS, HD), grad
 
 

time: 84 us -> 76 us (0.905)
  Pallas kernels: 78.2 us -> 72.4 us
  local copies, waits for them, and re-layouts: 4.98 us -> 2.84 us
    pallas_call x1, Pallas kernels: 78.2 us -> 71.1 us  [local(): pl.pallas_call(kernel, out_shape=(jax.ShapeDtypeStruct((HEADS, SPOTS, HD)...]
    transpose x1 -> x0, local copies, waits for them, and re-layouts: 3.41 us -> none  [local(): mixed.reshape(HEADS, CHUNKS, FRAMES, PART, HD).transpose(2, 1, 3, 0, 4)]
    unnamed x1 -> x6, local copies, waits for them, and re-layouts: 1.57 us -> 2.84 us
    pallas_call x0 -> x1, Pallas kernels: none -> 1.22 us  [local(): pl.pallas_call(write_out, out_shape=(jax.ShapeDtypeStruct((FRAMES, CHUNKS...]
where the time goes in v3:
time: 76 us; the launch traced here: 75.8 us
  Pallas kernels  72.4 us (95%)
  local copies, waits for them, and re-layouts  2.84 us (4%)
    pallas_call x1, Pallas kernels, local(): pl.pallas_call(kernel, out_shape=(jax.ShapeDtypeStruct((HEADS, SPOTS, HD)...  71.1 us
    unnamed x6, local copies, waits for them, and re-layouts  2.84 us

profile of v3, /device:TPU:1, one launch (start us, length us, event | category | flops | bytes accessed | tf_op | source)
XLA Modules:
  0.0 75.8 jit_solution(2381271031013449106)
XLA Ops:
  0.6 0.0 copy-start
  0.6 1.0 %copy-done = bf16[1,64,4096]{2,1,0:T(8,128)(2,1)S(1)} copy-done((bf16[1,64,4096]{2,1,0:T(8,128)(2,1)S(1)}, bf16[1,64,4096]{2,1,0:T(8,128)(2,1)}, u32[]{:S(2)}) %copy-start) | copy-done | bytes 524312
  1.7 0.0 copy-start.1
  1.7 0.9 %copy-done.1 = bf16[1,64,1024]{2,1,0:T(8,128)(2,1)S(1)} copy-done((bf16[1,64,1024]{2,1,0:T(8,128)(2,1)S(1)}, bf16[1,64,1024]{2,1,0:T(8,128)(2,1)}, u32[]{:S(2)}) %copy-start.1) | copy-done | bytes 131096
  2.6 0.0 copy-start.2
  2.6 0.9 %copy-done.2 = bf16[1,64,1024]{2,1,0:T(8,128)(2,1)S(1)} copy-done((bf16[1,64,1024]{2,1,0:T(8,128)(2,1)S(1)}, bf16[1,64,1024]{2,1,0:T(8,128)(2,1)}, u32[]{:S(2)}) %copy-start.2) | copy-done | bytes 131096
  3.5 71.1 %block.1 = (bf16[16,256,128]{2,1,0:T(8,128)(2,1)S(1)}, f32[8,4096]{1,0:T(8,128)S(1)}) custom-call(bf16[16,4,4,16,128]{4,3,2,1,0:T(8,128)(2,1)} %bitcast.12, bf16[16,4,4,16,128]{4,3,2,1,0:T(8,128)(2,1)} %bitcast.13, bf16[16,4,4,16,128]{4,3,2,1,0:T(8,128)(2,1)} %bitcast.14, bf16[16,4,4,16,128]{4,3,2,1,0:T(8,128)(2,1)} %bitcast.15, ...), custom_call_target="tpu_custom_call" | custom-call | tf_op jit(solution)/shard_map/block/pallas_call | solution.py:345
  74.6 1.2 %write_out.1 = (bf16[16,4,4,16,128]{4,3,2,1,0:T(8,128)(2,1)}, f32[8,4096]{1,0:T(8,128)}) custom-call(bf16[16,256,128]{2,1,0:T(8,128)(2,1)S(1)} %get-tuple-element.6.out_heads, f32[8,4096]{1,0:T(8,128)S(1)} %get-tuple-element.7.rows), custom_call_target="tpu_custom_call" | custom-call | tf_op jit(solution)/shard_map/write_out/pallas_call | solution.py:390
Async XLA Ops:
  0.6 1.0 %copy-start = (bf16[1,64,4096]{2,1,0:T(8,128)(2,1)S(1)}, bf16[1,64,4096]{2,1,0:T(8,128)(2,1)}, u32[]{:S(2)}) copy-start(bf16[1,64,4096]{2,1,0:T(8,128)(2,1)} %param.16) | copy-start | bytes 1572868
  1.7 0.9 %copy-start.1 = (bf16[1,64,1024]{2,1,0:T(8,128)(2,1)S(1)}, bf16[1,64,1024]{2,1,0:T(8,128)(2,1)}, u32[]{:S(2)}) copy-start(bf16[1,64,1024]{2,1,0:T(8,128)(2,1)} %param.14) | copy-start | bytes 393220
  2.6 0.9 %copy-start.2 = (bf16[1,64,1024]{2,1,0:T(8,128)(2,1)S(1)}, bf16[1,64,1024]{2,1,0:T(8,128)(2,1)}, u32[]{:S(2)}) copy-start(bf16[1,64,1024]{2,1,0:T(8,128)(2,1)} %param.15) | copy-start | bytes 393220

commit v4 on v3

--- a/solution.py
+++ b/solution.py
@@ -83,10 +83,10 @@
         pl.semaphore_signal(barrier, inc=1, device_id=device, device_id_type=MESH)
 
     def greet_seq(step, carry):
-        greet((dp, seq_peer(step)))
-        return carry
-
-    lax.fori_loop(0, 15, greet_seq, 0)
+        greet((dp, (me + step) % 16))
+        return carry
+
+    lax.fori_loop(1, 16, greet_seq, 0)
 
     def greet_y(step, carry):
         y_, c_ = y_peer(step)
@@ -96,6 +96,39 @@
     lax.fori_loop(2, 8, greet_y, 0)
     greet(at((x + 1) % 4, y, z, core))
     greet(at((x + 3) % 4, y, z, core))
+    pl.semaphore_wait(barrier, 23)
+
+    mine = audio.at[me // 2, core]
+    send(audio_now, mine, aud_send.at[0], aud_recv.at[0], at((x + 2) % 4, y, z, core))
+    for d in (1, 3, 2):
+        send(audio_now, mine, aud_send.at[0], aud_recv.at[1], at(x, y, (z + d) % 4, core))
+
+    def send_qkv(c, steps):
+        def one(peer):
+            for t, ref in enumerate((q_time, k_time, v_time)):
+                send(ref.at[peer, c], arrived.at[c, t, me], qkv_send.at[t], qkv_recv.at[c], (dp, peer))
+
+        def body(step, carry):
+            one(seq_peer(step))
+            return carry
+
+        lax.fori_loop(steps[0], steps[1], body, 0)
+
+    send_qkv(0, (0, 2))
+    send_qkv(1, (0, 2))
+    send_qkv(2, (0, 2))
+    send_qkv(3, (0, 2))
+    def send_y(step, carry):
+        y_, c_ = y_peer(step)
+        to = at(x, y_, z, c_)
+        cols = pl.ds(pl.multiple_of((y_ * 2 + c_) * 512, 512), 512)
+        send(cotangent.at[:, cols], cotan.at[line], grad_send.at[1], grad_recv.at[1], to)
+        return carry
+
+    for d in (1, 3, 2):
+        send(audio_earlier, earlier.at[y, core], grad_send.at[0], grad_recv.at[0], at(x, (y + d) % 4, z, core))
+    lax.fori_loop(1, 8, send_y, 0)
+
     for c in range(CHUNKS):
         local(q_space.at[:, c], q_raw.at[c], local_sem.at[0])
         local(k_space.at[:, c], k_raw.at[c], local_sem.at[1])
@@ -106,37 +139,6 @@
     local(audio_earlier, earlier.at[y, core], grad_recv.at[0])
     local(cotangent.at[:, pl.ds(pl.multiple_of(line * 512, 512), 512)], cotan.at[line], grad_recv.at[1])
 
-    pl.semaphore_wait(barrier, 23)
-
-    mine = audio.at[me // 2, core]
-    send(audio_now, mine, aud_send.at[0], aud_recv.at[0], at((x + 2) % 4, y, z, core))
-    for d in (1, 3, 2):
-        send(audio_now, mine, aud_send.at[0], aud_recv.at[1], at(x, y, (z + d) % 4, core))
-
-    def send_qkv(c, steps):
-        def one(peer):
-            for t, ref in enumerate((q_time, k_time, v_time)):
-                send(ref.at[peer, c], arrived.at[c, t, me], qkv_send.at[t], qkv_recv.at[c], (dp, peer))
-
-        def body(step, carry):
-            one(seq_peer(step))
-            return carry
-
-        lax.fori_loop(steps[0], steps[1], body, 0)
-
-    send_qkv(0, (0, 2))
-    send_qkv(1, (0, 2))
-    def send_y(step, carry):
-        y_, c_ = y_peer(step)
-        to = at(x, y_, z, c_)
-        cols = pl.ds(pl.multiple_of((y_ * 2 + c_) * 512, 512), 512)
-        send(cotangent.at[:, cols], cotan.at[line], grad_send.at[1], grad_recv.at[1], to)
-        return carry
-
-    for d in (1, 3, 2):
-        send(audio_earlier, earlier.at[y, core], grad_send.at[0], grad_recv.at[0], at(x, (y + d) % 4, z, core))
-    lax.fori_loop(1, 8, send_y, 0)
-
     row = lax.broadcasted_iota(jnp.int32, (256, 256), 0)
     col = lax.broadcasted_iota(jnp.int32, (256, 256), 1)
     bias[...] = jnp.where(row % 16 == col % 16, 0.0, NEG).astype(F32)
@@ -170,7 +172,7 @@
         wait(arrived.at[c], qkv_recv.at[c])
 
         def attend(i, carry):
-            for s in (2 * i, 2 * i + 1):
+            for s in range(PART):
                 queries = arrived[c, 0, :, s].reshape(256, HD)
                 key_rows = arrived[c, 1, :, s].reshape(256, HD)
                 values = arrived[c, 2, :, s].reshape(256, HD)
@@ -179,7 +181,7 @@
                 back[c, :, s] = result.astype(BF16).reshape(FRAMES, HEADS, HD)
             return carry
 
-        lax.fori_loop(0, PART // 2, attend, 0)
+        lax.fori_loop(0, 1, attend, 0)
 
         def go(step, carry):
             peer = seq_peer(step)
@@ -237,23 +239,25 @@
     send(part_x.at[(x + 2) % 4, late], relay.at[1], grad_send.at[2], grad_recv.at[2], to_left)
     send(part_x.at[right, late], from_x.at[0, late], grad_send.at[2], grad_recv.at[6], to_right)
     send(part_x.at[left, early], from_x.at[1, early], grad_send.at[2], grad_recv.at[6], to_left)
+    send_qkv(2, (2, 15))
     wait(audio_now, local_sem.at[3])
     wait(audio.at[pl.ds(0, 6), 0], aud_recv.at[1])
     side = audio.at[:, core]
     send(side, side, aud_send.at[1], aud_recv.at[2], at(x, y, z, 1 - core))
-    send_qkv(2, (0, 15))
+    wait(w_vmem, local_sem.at[2])
+    wait(audio.at[:, 0], aud_recv.at[2])
+    lax.fori_loop(0, 2, audio_pair, 0)
     temporal(0)
     wait(relay, grad_recv.at[2])
     merged[0] = (part_x[right, early].astype(F32) + relay[0].astype(F32)).astype(BF16)
     merged[1] = (part_x[left, late].astype(F32) + relay[1].astype(F32)).astype(BF16)
     send(merged.at[0], from_x.at[0, early], grad_send.at[6], grad_recv.at[6], to_right)
     send(merged.at[1], from_x.at[1, late], grad_send.at[6], grad_recv.at[6], to_left)
-    wait(w_vmem, local_sem.at[2])
-    wait(audio.at[:, 0], aud_recv.at[2])
-    lax.fori_loop(0, 3, audio_pair, 0)
+    lax.fori_loop(2, 4, audio_pair, 0)
+    send_qkv(3, (2, 8))
     temporal(1)
-    send_qkv(3, (0, 15))
-    lax.fori_loop(3, 6, audio_pair, 0)
+    send_qkv(3, (8, 15))
+    lax.fori_loop(4, 6, audio_pair, 0)
     wait(from_x, grad_recv.at[6])
     for z_ in range(4):
         total = part_x[x, z_].astype(F32) + from_x[0, z_].astype(F32) + from_x[1, z_].astype(F32)

time: 76 us -> 75.9 us (level)
  no operation moved by 1% of the time
where the time goes in v4:
time: 75.9 us; the launch traced here: 75.8 us
  Pallas kernels  72.3 us (95%)
  local copies, waits for them, and re-layouts  2.84 us (4%)
    pallas_call x1, Pallas kernels, local(): pl.pallas_call(kernel, out_shape=(jax.ShapeDtypeStruct((HEADS, SPOTS, HD)...  71 us
    unnamed x6, local copies, waits for them, and re-layouts  2.84 us

profile of v4, /device:TPU:1, one launch (start us, length us, event | category | flops | bytes accessed | tf_op | source)
XLA Modules:
  0.0 75.8 jit_solution(11349280502210638576)
XLA Ops:
  0.6 0.0 copy-start
  0.6 1.0 %copy-done = bf16[1,64,4096]{2,1,0:T(8,128)(2,1)S(1)} copy-done((bf16[1,64,4096]{2,1,0:T(8,128)(2,1)S(1)}, bf16[1,64,4096]{2,1,0:T(8,128)(2,1)}, u32[]{:S(2)}) %copy-start) | copy-done | bytes 524312
  1.7 0.0 copy-start.1
  1.7 0.9 %copy-done.1 = bf16[1,64,1024]{2,1,0:T(8,128)(2,1)S(1)} copy-done((bf16[1,64,1024]{2,1,0:T(8,128)(2,1)S(1)}, bf16[1,64,1024]{2,1,0:T(8,128)(2,1)}, u32[]{:S(2)}) %copy-start.1) | copy-done | bytes 131096
  2.6 0.0 copy-start.2
  2.6 0.9 %copy-done.2 = bf16[1,64,1024]{2,1,0:T(8,128)(2,1)S(1)} copy-done((bf16[1,64,1024]{2,1,0:T(8,128)(2,1)S(1)}, bf16[1,64,1024]{2,1,0:T(8,128)(2,1)}, u32[]{:S(2)}) %copy-start.2) | copy-done | bytes 131096
  3.5 71.0 %block.1 = (bf16[16,256,128]{2,1,0:T(8,128)(2,1)S(1)}, f32[8,4096]{1,0:T(8,128)S(1)}) custom-call(bf16[16,4,4,16,128]{4,3,2,1,0:T(8,128)(2,1)} %bitcast.12, bf16[16,4,4,16,128]{4,3,2,1,0:T(8,128)(2,1)} %bitcast.13, bf16[16,4,4,16,128]{4,3,2,1,0:T(8,128)(2,1)} %bitcast.14, bf16[16,4,4,16,128]{4,3,2,1,0:T(8,128)(2,1)} %bitcast.15, ...), custom_call_target="tpu_custom_call" | custom-call | tf_op jit(solution)/shard_map/block/pallas_call | solution.py:349
  74.5 1.2 %write_out.1 = (bf16[16,4,4,16,128]{4,3,2,1,0:T(8,128)(2,1)}, f32[8,4096]{1,0:T(8,128)}) custom-call(bf16[16,256,128]{2,1,0:T(8,128)(2,1)S(1)} %get-tuple-element.6.out_heads, f32[8,4096]{1,0:T(8,128)S(1)} %get-tuple-element.7.rows), custom_call_target="tpu_custom_call" | custom-call | tf_op jit(solution)/shard_map/write_out/pallas_call | solution.py:394
Async XLA Ops:
  0.6 1.0 %copy-start = (bf16[1,64,4096]{2,1,0:T(8,128)(2,1)S(1)}, bf16[1,64,4096]{2,1,0:T(8,128)(2,1)}, u32[]{:S(2)}) copy-start(bf16[1,64,4096]{2,1,0:T(8,128)(2,1)} %param.16) | copy-start | bytes 1572868
  1.7 0.9 %copy-start.1 = (bf16[1,64,1024]{2,1,0:T(8,128)(2,1)S(1)}, bf16[1,64,1024]{2,1,0:T(8,128)(2,1)}, u32[]{:S(2)}) copy-start(bf16[1,64,1024]{2,1,0:T(8,128)(2,1)} %param.14) | copy-start | bytes 393220
  2.6 0.9 %copy-start.2 = (bf16[1,64,1024]{2,1,0:T(8,128)(2,1)S(1)}, bf16[1,64,1024]{2,1,0:T(8,128)(2,1)}, u32[]{:S(2)}) copy-start(bf16[1,64,1024]{2,1,0:T(8,128)(2,1)} %param.15) | copy-start | bytes 393220
